TPU v7x, 512 devices: a whole 4x8x8 slice. The times are simulated.
512 devices in a mesh: sec: 2 (over core), seq: 32 (over y, x), tp: 8 (over z).
Axes of the slice: x: 4, y: 8, z: 8, core: 2. Of those that a mesh axis runs over, the one named last changes fastest.
Arguments:
- hidden_rows: bfloat16 [2, 2048, 5120], P('sec', 'seq'), may hold values from -10 to 10
- carried: bfloat16 [2, 2048, 5120], P('sec', 'seq'), may hold values from -6 to 6
- query_weight: bfloat16 [2, 5120, 4096], P('sec', 'seq', 'tp'), may hold values from -6 to 6
- response_cache: bfloat16 [2, 2048, 2048], P('sec', 'seq', 'tp'), may hold values from -8.375 to 8.375
- prompt_cache: bfloat16 [2, 8, 16384, 2048], P('sec', None, 'seq', 'tp'), may hold values from -5 to 5
- prompt_lengths: int32 [8], replicated, may hold values from 1 to 16384, 81920 in all
- response_lengths: int32 [2, 32], replicated, may hold values from 1 to 64, 1280 in all within a row
- block_prompts: int32 [2, 32, 1], replicated, may hold values from 0 to 7
Outputs:
- attended: bfloat16 [2, 2048, 4096], P('sec', 'seq', 'tp')
All inputs are finite; a program needn't handle non-finite values.
Results may differ from a plain program's by a relative error of at most 0.0096.
Values may be sent and summed in bfloat16 or wider, within the bound.
A program may use at most 64 MiB of HBM per device.

v0:
```python
import math

import jax
import jax.numpy as jnp
from jax import lax
from jax.sharding import PartitionSpec as P

H = 32
KVH = 8
HD = 128


NEG_FILL = -1e30


def from_behind(value, axis, steps):
    count = lax.axis_size(axis)
    first, last = (max(0, -steps), min(count, count - steps))
    return lax.ppermute(value, axis, [(source, source + steps) for source in range(first, last)])


def partial_attend(queries, key_rows, value_rows, key_valid):
    score_scale = queries.shape[-1] ** (-0.5)
    scores = (
        jnp.einsum("rgqd,kgd->rgqk", queries, key_rows, preferred_element_type=jnp.float32)
        * score_scale
    )
    key_mask = key_valid[:, None, None, :]
    row_peak = jnp.max(jnp.where(key_mask, scores, NEG_FILL), axis=-1)
    weights = jnp.where(key_mask, jnp.exp(scores - row_peak[..., None]), 0.0).astype(jnp.bfloat16)
    row_total = jnp.sum(weights.astype(jnp.float32), axis=-1)
    row_sum = jnp.einsum("rgqk,kgd->rgqd", weights, value_rows, preferred_element_type=jnp.float32)
    return (row_peak, row_total, row_sum)


def shards(
    hidden_rows,
    carried,
    query_weight,
    response_cache,
    prompt_cache,
    prompt_lengths,
    response_lengths,
    block_prompts,
):
    section = lax.axis_index("sec")
    shard_index = lax.axis_index("seq")
    shard_count = lax.axis_size("seq")
    rows = hidden_rows.shape[1]
    local_kv = response_cache.shape[2] // (2 * HD)
    ratio = H // KVH
    handed = from_behind(carried, "sec", 1)
    inputs = (hidden_rows[0].astype(jnp.float32) + handed[0].astype(jnp.float32)).astype(
        jnp.bfloat16
    )
    projected = jnp.dot(
        inputs,
        lax.all_gather(query_weight[0], "seq", axis=0, tiled=True),
        preferred_element_type=jnp.float32,
    )
    queries = projected.astype(jnp.bfloat16).reshape(rows, local_kv, ratio, HD)
    own_cache = response_cache[0].reshape(rows, local_kv, 2, HD)
    order = jnp.arange(rows, dtype=jnp.int32)
    causal = order[:, None] >= order[None, :]
    own_part = partial_attend(queries, own_cache[:, :, 0], own_cache[:, :, 1], causal)
    section_prompts = lax.dynamic_index_in_dim(block_prompts, section, 0, keepdims=False)[:, 0]
    section_lengths = lax.dynamic_index_in_dim(response_lengths, section, 0, keepdims=False)
    my_length = section_lengths[shard_index]
    prompt_tiles = prompt_cache[0]
    tile_len = prompt_tiles.shape[1]
    gathered = lax.all_gather(queries, "seq", axis=0, tiled=True)
    group = math.gcd(shard_count, 4)
    grouped_queries = gathered.reshape(shard_count // group, group, rows, local_kv, ratio, HD)
    grouped_prompts = section_prompts.reshape(shard_count // group, group)
    positions = shard_index * tile_len + jnp.arange(tile_len, dtype=jnp.int32)

    def tile_parts(tile_inputs):
        group_queries, group_prompts = tile_inputs
        group_cache = jnp.take(prompt_tiles, group_prompts, axis=0).reshape(
            group, tile_len, local_kv, 2, HD
        )
        key_valid = (positions[None, :] < prompt_lengths[group_prompts][:, None])[:, None, :]
        return jax.vmap(partial_attend)(
            group_queries, group_cache[:, :, :, 0], group_cache[:, :, :, 1], key_valid
        )

    parts = lax.map(tile_parts, (grouped_queries, grouped_prompts))
    peaks = parts[0].reshape((shard_count,) + parts[0].shape[2:])
    totals = parts[1].reshape((shard_count,) + parts[1].shape[2:])
    sums = parts[2].reshape((shard_count,) + parts[2].shape[2:])
    returned = (
        lax.all_to_all(peaks, "seq", split_axis=0, concat_axis=0, tiled=True),
        lax.all_to_all(totals, "seq", split_axis=0, concat_axis=0, tiled=True),
        lax.all_to_all(sums, "seq", split_axis=0, concat_axis=0, tiled=True),
    )
    row_peak = jnp.maximum(own_part[0], jnp.max(returned[0], axis=0))
    own_scale = jnp.exp(own_part[0] - row_peak)
    far_scale = jnp.exp(returned[0] - row_peak[None])
    merged = (
        row_peak,
        own_part[1] * own_scale + jnp.sum(returned[1] * far_scale, axis=0),
        own_part[2] * own_scale[..., None] + jnp.sum(returned[2] * far_scale[..., None], axis=0),
    )
    output = merged[2] / merged[1][..., None]
    output = jnp.where((order < my_length)[:, None, None, None], output, 0.0)
    return output.reshape(1, rows, local_kv * ratio * HD).astype(jnp.bfloat16)


def solution(mesh):
    placed = (
        P("sec", "seq", None),
        P("sec", "seq", None),
        P("sec", "seq", "tp"),
        P("sec", "seq", "tp"),
        P("sec", None, "seq", "tp"),
        P(),
        P(),
        P(),
    )
    return jax.shard_map(
        shards, mesh=mesh, in_specs=placed, out_specs=P("sec", "seq", "tp"), check_vma=False
    )
```

profile of v0, /device:TPU:6, one launch (start us, length us, event | category | flops | bytes accessed | tf_op | source)
XLA Modules:
  0.0 386.5 jit_solution(14329077157300811704)
XLA Ops:
  6.5 0.7 all-gather.6.cloned.1.call-update
  7.3 1.8 collective-permute-start
  9.1 1.9 collective-permute-done
  11.0 92.6 %all-gather.6.cloned.1.call-done = bf16[1,5120,512]{2,1,0:T(8,128)(2,1)} async-done(((bf16[1,160,512]{2,1,0:T(8,128)(2,1)}), bf16[1,5120,512]{2,1,0:T(8,128)(2,1)}) %all-gather.6.cloned.1.call-update) | async-done | bytes 5242896 | tf_op jit(solution)/shard_map/all_gather | solution.py:58
  103.6 3.6 fusion.22
  108.1 81.4 %all-gather.4.cloned.1.call-done = bf16[2048,1,4,128]{3,0,2,1:T(8,128)(2,1)} async-done(((bf16[64,1,4,128]{3,0,2,1:T(8,128)(2,1)}), bf16[2048,1,4,128]{3,0,2,1:T(8,128)(2,1)}) %all-gather.4.cloned.1.call-update) | async-done | bytes 2097168 | tf_op jit(solution)/shard_map/all_gather | solution.py:71
  189.4 63.0 %while.16 = (s32[]{:T(128)}, f32[8,4,64,1,4]{2,4,1,3,0:T(4,128)S(1)}, f32[8,4,64,1,4]{2,4,3,1,0:T(4,128)S(1)}, f32[8,4,64,1,4,128]{5,2,4,1,3,0:T(8,128)}, s32[8,...) while((s32[]{:T(128)}, ...), condition=%wide.region_4.5_spmd.clone.clone, body=%wide.region_1.4_spmd.clone.sunk.clone | while | flops 275777056 | bytes 16585993 | solution.py:87
  189.4 2.2 gather_fusion.1
  192.2 0.7 copy.72
  193.8 1.5 fusion.44
  195.3 1.3 fusion.45
  197.3 2.2 gather_fusion.1
  200.1 0.7 copy.72
  201.6 1.5 fusion.44
  203.1 1.4 fusion.45
  205.2 2.2 gather_fusion.1
  207.9 0.7 copy.72
  209.5 1.5 fusion.44
  211.0 1.4 fusion.45
  213.1 2.2 gather_fusion.1
  215.8 0.7 copy.72
  217.4 1.5 fusion.44
  218.9 1.4 fusion.45
  221.0 2.2 gather_fusion.1
  223.7 0.7 copy.72
  225.3 1.5 fusion.44
  226.8 1.4 fusion.45
  228.8 2.2 gather_fusion.1
  231.6 0.7 copy.72
  233.2 1.5 fusion.44
  234.6 1.4 fusion.45
  236.7 2.2 gather_fusion.1
  239.5 0.7 copy.72
  241.1 1.5 fusion.44
  242.5 1.3 fusion.45
  244.6 2.2 gather_fusion.1
  247.3 0.7 copy.72
  248.9 1.5 fusion.44
  250.4 1.4 fusion.45
  252.4 0.7 reshape.275
  253.1 7.4 %all-to-all-start = ((f32[32,1,256]{2,1,0:T(1,128)}), f32[32,1,256]{2,1,0:T(1,128)S(1)}, u32[]{:S(2)}, u32[]{:S(2)}) async-start(f32[32,1,256]{2,1,0:T(1,128)} %reshape.275), calls=%async_computation | async-start | bytes 65536 | tf_op jit(solution)/shard_map/all_to_all | solution.py:92
  260.7 8.0 %all-to-all-done = f32[32,1,256]{2,1,0:T(1,128)S(1)} async-done(((f32[32,1,256]{2,1,0:T(1,128)}), f32[32,1,256]{2,1,0:T(1,128)S(1)}, u32[]{:S(2)}, u32[]{:S(2)}) %all-to-all-start) | async-done | bytes 32800 | tf_op jit(solution)/shard_map/all_to_all | solution.py:92
  268.7 12.8 %all_to_all.15 = f32[32,1,256]{2,1,0:T(1,128)S(1)} all-to-all(f32[32,1,256]{2,1,0:T(1,128)S(1)} %reshape.277), channel_id=1, replica_groups=mesh['sec'=2,'seq'=32,'tp'=8] {'seq'}, dimensions={0} | all-to-all | bytes 65536 | tf_op jit(solution)/shard_map/all_to_all | solution.py:93
  281.5 6.5 %all-to-all-start.1 = ((f32[32,64,1,4,128]{4,1,3,2,0:T(8,128)}), f32[32,64,1,4,128]{4,1,3,2,0:T(8,128)}, u32[]{:S(2)}, u32[]{:S(2)}) async-start(f32[32,64,1,4,128]{4,1,3,2,0:T(8,128)} %bitcast.194), calls=%async_computation.1 | async-start | bytes 8388608 | tf_op jit(solution)/shard_map/all_to_all | solution.py:94
  290.1 0.7 reduce.12
  291.0 0.7 reduce.13
  291.9 84.0 %all-to-all-done.1 = f32[32,64,1,4,128]{4,1,3,2,0:T(8,128)} async-done(((f32[32,64,1,4,128]{4,1,3,2,0:T(8,128)}), f32[32,64,1,4,128]{4,1,3,2,0:T(8,128)}, u32[]{:S(2)}, u32[]{:S(2)}) %all-to-all-start.1) | async-done | bytes 4194336 | tf_op jit(solution)/shard_map/all_to_all | solution.py:94
  375.9 2.9 multiply_reduce_fusion
  (124 shorter events, 21.1 us)
Async XLA Ops:
  6.5 101.4 %copy-start = (s32[2,32,1]{1,2,0:T(1,128)S(1)}, s32[2,32,1]{1,2,0:T(1,128)}, u32[]{:S(2)}) copy-start(s32[2,32,1]{1,2,0:T(1,128)} %param.17) | copy-start | bytes 772
  6.5 97.1 %all-gather.6.cloned.1.call-start = ((), (), s32[]{:S(2)}) async-start(), calls=%async_computation.4 | async-start | bytes 5406720 | tf_op jit(solution)/shard_map/all_gather | solution.py:58
  7.3 182.2 %copy-start.1 = (s32[8]{0:T(128)S(1)}, s32[8]{0:T(128)}, u32[]{:S(2)}) copy-start(s32[8]{0:T(128)} %param.15) | copy-start | bytes 100
  7.3 182.1 %all-gather.4.cloned.1.call-start = ((), (), s32[]{:S(2)}) async-start(), calls=%async_computation.3 | async-start | bytes 2162688 | tf_op jit(solution)/shard_map/all_gather | solution.py:71
  7.3 3.7 collective-permute-start
  253.1 15.6 %all-to-all-start = ((f32[32,1,256]{2,1,0:T(1,128)}), f32[32,1,256]{2,1,0:T(1,128)S(1)}, u32[]{:S(2)}, u32[]{:S(2)}) async-start(f32[32,1,256]{2,1,0:T(1,128)} %reshape.275), calls=%async_computation | async-start | bytes 65536 | tf_op jit(solution)/shard_map/all_to_all | solution.py:92
  281.5 6.5 %copy-start.2 = (bf16[1,64,256]{2,1,0:T(8,128)(2,1)S(1)}, bf16[1,64,256]{2,1,0:T(8,128)(2,1)}, u32[]{:S(2)}) copy-start(bf16[1,64,256]{2,1,0:T(8,128)(2,1)} %param.13) | copy-start | bytes 98308
  281.5 6.5 %copy-start.3 = (s32[2,32]{1,0:T(2,128)S(1)}, s32[2,32]{1,0:T(2,128)}, u32[]{:S(2)}) copy-start(s32[2,32]{1,0:T(2,128)} %param.16) | copy-start | bytes 772
  281.5 94.4 %all-to-all-start.1 = ((f32[32,64,1,4,128]{4,1,3,2,0:T(8,128)}), f32[32,64,1,4,128]{4,1,3,2,0:T(8,128)}, u32[]{:S(2)}, u32[]{:S(2)}) async-start(f32[32,64,1,4,128]{4,1,3,2,0:T(8,128)} %bitcast.194), calls=%async_computation.1 | async-start | bytes 8388608 | tf_op jit(solution)/shard_map/all_to_all | solution.py:94
Sparse Core Ops, SparseCore 0:
  10.5 93.0 all-gather.5
  108.0 81.3 all-gather.3
where the time goes:
time: 389 us; the launch traced here: 387 us
  waiting for transfers between devices  269 us (69%)
  local copies, waits for them, and re-layouts  36.3 us (9%)
  matrix products  26.7 us (7%)
  starting transfers between devices  15.7 us (4%)
  between operations  13.6 us (3%)
  blocking collectives  12.8 us (3%)
  other arithmetic  12.3 us (3%)
    all_gather x1, waiting for transfers between devices, shards(): lax.all_gather(query_weight[0], 'seq', axis=0, tiled=True)  92.6 us
    all_to_all x1, waiting for transfers between devices, shards(): lax.all_to_all(sums, 'seq', split_axis=0, concat_axis=0, tiled=True)  84 us
    all_gather x1, waiting for transfers between devices, shards(): gathered = lax.all_gather(queries, 'seq', axis=0, tiled=True)  81.4 us
    gather x24, local copies, waits for them, and re-layouts, tile_parts(): jnp.take(prompt_tiles, group_prompts, axis=0)  27.3 us
    all_to_all x1, blocking collectives, shards(): lax.all_to_all(totals, 'seq', split_axis=0, concat_axis=0, tiled=True)  12.8 us
    dot_general x9, matrix products, partial_attend(): jnp.einsum('rgqd,kgd->rgqk', queries, key_rows, preferred_element_type=jn...  12 us
    dot_general x9, matrix products, partial_attend(): jnp.einsum('rgqk,kgd->rgqd', weights, value_rows, preferred_element_type=...  11.1 us
    all_to_all x1, waiting for transfers between devices, shards(): lax.all_to_all(peaks, 'seq', split_axis=0, concat_axis=0, tiled=True)  8.04 us
  transfers between devices with their start and end apart: 5, of which 5 were waited for; matrix products, arithmetic and copies ran while one was open for 1% of the time, Pallas kernels for 0%

commit v1 on v0

v1 whole, which is shorter than its diff:
```python
import jax
import jax.numpy as jnp
from jax import lax
from jax.experimental import pallas as pl
from jax.experimental.pallas import tpu as pltpu
from jax.sharding import PartitionSpec as P

MESH = pl.DeviceIdType.MESH
HD = 128
NP = 8
TILE = 512
NX, NY = 4, 8
BL = 64
DEPTH = 160
WIDE = DEPTH * NY
COLS = 512
LANES = 256
HALF = 128
PAY = 144
SUB = DEPTH // 2
NEG = -1e30
SCALE = HD**-0.5 * 1.4426950408889634
F32 = jnp.float32
BF16 = jnp.bfloat16


def slot(rx, ry):
    return lax.rem(ry + NY, NY) * NX + rx if not isinstance(ry, int) else (ry % NY) * NX + rx


def kernel(
    bp,
    plen,
    rlen,
    hid_h,
    car_h,
    w_h,
    rc_h,
    kv_h,
    out,
    hid,
    handed,
    xin,
    lhs,
    wbuf,
    pbuf,
    prec,
    kv,
    rc,
    vt,
    q,
    own,
    mine,
    send_a,
    send_b,
    ra_y,
    ra_x,
    rb_y,
    rb_x,
    local_sem,
    hand_s,
    hand_r,
    xin_s,
    xin_r,
    w_s,
    w_r,
    p_s,
    p_r,
    qay_s,
    qay_r,
    qax_s,
    qax_r,
    qby_s,
    qby_r,
    qbx_s,
    qbx_r,
    oay_s,
    oay_r,
    oax_s,
    oax_r,
    oby_s,
    oby_r,
    obx_s,
    obx_r,
):
    sec = lax.axis_index("sec")
    seq = lax.axis_index("seq")
    y, x = seq // NX, lax.rem(seq, NX)
    turn = 1 - 2 * sec

    def at_x(rx):
        return lax.rem(x + turn * rx + 2 * NX, NX)

    def at_y(ry):
        return lax.rem(y + turn * ry + 2 * NY, NY)

    def dev(rx, ry):
        return at_y(ry) * NX + at_x(rx)

    xp, xm, x2 = dev(1, 0), dev(-1, 0), dev(2, 0)
    yp, ym = dev(0, 1), dev(0, -1)
    drains = []

    def copy(src, dst, ss, rs, where):
        return pltpu.make_async_remote_copy(
            src_ref=src,
            dst_ref=dst,
            send_sem=ss,
            recv_sem=rs,
            device_id={"seq": where},
            device_id_type=MESH,
        )

    def push(src, dst, ss, rs, where):
        c = copy(src, dst, ss, rs, where)
        c.start()
        drains.append(c.wait_send)

    def got(dst, rs):
        copy(dst, dst, rs, rs, xp).wait_recv()

    in_hid = pltpu.make_async_copy(hid_h.at[0], hid, local_sem.at[0])
    in_kv = pltpu.make_async_copy(kv_h.at[0], kv, local_sem.at[1])
    in_rc = pltpu.make_async_copy(rc_h.at[0], rc, local_sem.at[2])
    in_w = pltpu.make_async_copy(w_h.at[0], wbuf.at[y], local_sem.at[3])
    in_hid.start()
    in_w.start()
    in_kv.start()
    in_rc.start()

    barrier = pltpu.get_barrier_semaphore()
    for where in (xp, xm, x2, yp, ym):
        pl.semaphore_signal(barrier, inc=1, device_id={"seq": where}, device_id_type=MESH)
    pl.semaphore_signal(barrier, inc=1, device_id={"sec": 1 - sec}, device_id_type=MESH)
    pl.semaphore_wait(barrier, 6)

    hand = pltpu.make_async_remote_copy(
        src_ref=car_h.at[0],
        dst_ref=handed,
        send_sem=hand_s,
        recv_sem=hand_r,
        device_id={"sec": 1 - sec},
        device_id_type=MESH,
    )

    @pl.when(sec == 0)
    def _():
        hand.start()

    def w_part(ry, sub):
        return wbuf.at[at_y(ry), pl.ds(sub * SUB, SUB), :]

    for sub in range(2):
        part = w_h.at[0, pl.ds(sub * SUB, SUB), :]
        push(part, w_part(0, sub), w_s.at[0, 0, sub], w_r.at[0, 0, sub], yp)
        push(part, w_part(0, sub), w_s.at[1, 0, sub], w_r.at[1, 0, sub], ym)

    @pl.when(sec == 0)
    def _():
        handed[...] = jnp.zeros_like(handed)

    @pl.when(sec == 1)
    def _():
        hand.wait_recv()

    in_hid.wait()

    def regroup(r, carry):
        rows = pl.ds(pl.multiple_of(r * 16, 16), 16)
        lane = lax.broadcasted_iota(jnp.int32, (16, 4 * DEPTH), 1)
        for g in range(2):
            parts = []
            for j in range(4):
                cols = pl.ds(4 * DEPTH * (4 * g + j), 4 * DEPTH)
                v = hid[rows, cols].astype(F32) + handed[rows, cols].astype(F32)
                parts.append(v.astype(BF16).astype(F32))
            for xx in range(NX):
                total = None
                for j in range(4):
                    shift = (DEPTH * (j - xx)) % (4 * DEPTH)
                    v = parts[j] if shift == 0 else pltpu.roll(parts[j], shift, 1)
                    total = v if total is None else jnp.where(lane >= DEPTH * j, v, total)
                xin[xx, rows, pl.ds(4 * DEPTH * g, 4 * DEPTH)] = total.astype(BF16)
        return carry

    lax.fori_loop(0, BL // 16, regroup, 0)
    for n, (rx, where) in enumerate(((1, xp), (-1, xm), (2, x2))):
        push(xin.at[at_x(rx)], lhs.at[(-rx) % NX], xin_s.at[n], xin_r.at[n], where)
    lhs[0] = xin[x]

    in_kv.wait()

    def values_across(p, carry):
        vt[p, 0:HD, :] = kv[p, :, HD : 2 * HD].astype(F32).T.astype(BF16)
        vt[p, HD:PAY, :] = jnp.ones((PAY - HD, TILE), BF16)
        return carry

    for k in range(1, 5):
        for sub in range(2):
            got(w_part(-k, sub), w_r.at[0, k - 1, sub])
            if k < 4:
                part = w_part(-k, sub)
                push(part, part, w_s.at[0, k, sub], w_r.at[0, k, sub], yp)
                got(w_part(k, sub), w_r.at[1, k - 1, sub])
                if k < 3:
                    part = w_part(k, sub)
                    push(part, part, w_s.at[1, k, sub], w_r.at[1, k, sub], ym)
        if k < 4:
            lax.fori_loop(3 * k - 3, min(3 * k, NP), values_across, 0)

    in_w.wait()
    in_rc.wait()
    got(lhs.at[2], xin_r.at[2])
    got(lhs.at[3], xin_r.at[0])
    weight = wbuf[...].reshape(WIDE, COLS)
    far = jnp.dot(lhs[2:4].reshape(2 * BL, WIDE), weight, preferred_element_type=F32)
    pbuf[2:4] = far.reshape(2, BL, COLS)
    push(pbuf.at[2], prec.at[0], p_s.at[0], p_r.at[0], xp)
    push(pbuf.at[3], prec.at[2], p_s.at[2], p_r.at[2], xm)
    got(lhs.at[1], xin_r.at[1])
    near = jnp.dot(lhs[0:2].reshape(2 * BL, WIDE), weight, preferred_element_type=F32)
    pbuf[0:2] = near.reshape(2, BL, COLS)
    got(prec.at[0], p_r.at[0])
    pbuf[1] = pbuf[1] + prec[0]
    push(pbuf.at[1], prec.at[1], p_s.at[1], p_r.at[1], xp)
    got(prec.at[2], p_r.at[2])
    got(prec.at[1], p_r.at[1])
    mine_q = pbuf[0] + prec[1] + prec[2]
    for h in range(2):
        first = mine_q[:, 2 * h * HD : (2 * h + 1) * HD]
        second = mine_q[:, (2 * h + 1) * HD : (2 * h + 2) * HD]
        both = jnp.concatenate([first, second], axis=0)
        q[0, :, h * HALF : (h + 1) * HALF] = both.T.astype(BF16)

    def q_a(s):
        return q.at[s, :, pl.ds(0, HALF)]

    def q_b(s):
        return q.at[s, :, pl.ds(HALF, HALF)]

    def a_hop(arm, k, i):
        sign = -1 if arm == 0 else 1
        src, dst = slot(i, sign * (k - 1)), slot(i, sign * k)
        return copy(
            q_a(src),
            q_a(dst),
            qay_s.at[arm, k - 1, i],
            qay_r.at[arm, k - 1, i],
            yp if arm == 0 else ym,
        )

    def b_hop(arm, k):
        sign = -1 if arm == 0 else 1
        return copy(
            q_b(slot(0, sign * (k - 1))),
            q_b(slot(0, sign * k)),
            qby_s.at[arm, k - 1],
            qby_r.at[arm, k - 1],
            yp if arm == 0 else ym,
        )

    def b_side(n, ry):
        src, dst = ((0, 3), (0, 1), (3, 2))[n]
        return copy(
            q_b(slot(src, ry)),
            q_b(slot(dst, ry)),
            qbx_s.at[n, ry % NY],
            qbx_r.at[n, ry % NY],
            xm if n == 1 else xp,
        )

    def go(c):
        c.start()
        drains.append(c.wait_send)

    a_side = [
        copy(q_a(0), q_a(3), qax_s.at[0], qax_r.at[0], xp),
        copy(q_a(0), q_a(1), qax_s.at[1], qax_r.at[1], xm),
        copy(q_a(0), q_a(2), qax_s.at[2], qax_r.at[2], x2),
    ]
    for c in a_side:
        go(c)
    go(b_hop(0, 1))
    go(b_hop(1, 1))
    go(a_hop(0, 1, 0))
    go(a_hop(1, 1, 0))
    go(b_side(0, 0))
    go(b_side(1, 0))

    own_s = (
        jnp.dot(rc[:, 0:HD], q[0], preferred_element_type=F32) * SCALE
    )
    own_t = lax.broadcasted_iota(jnp.int32, (BL, LANES), 0)
    own_i = lax.rem(lax.broadcasted_iota(jnp.int32, (BL, LANES), 1), BL)
    own_s = jnp.where(own_t <= own_i, own_s, NEG)
    own_m = jnp.max(own_s, axis=0, keepdims=True)
    own_w = jnp.exp2(own_s - own_m).astype(BF16)
    own_v = rc[:, HD : 2 * HD].astype(F32).T.astype(BF16)
    mine[0:HD] = jnp.dot(own_v, own_w, preferred_element_type=F32)
    mine[HD : HD + 8] = jnp.broadcast_to(
        jnp.sum(own_w.astype(F32), axis=0, keepdims=True), (8, LANES)
    )
    mine[HD + 8 : PAY] = jnp.broadcast_to(own_m, (8, LANES))

    for c, i in ((a_side[1], 1), (a_side[2], 2), (a_side[0], 3)):
        c.wait_recv()
        go(a_hop(0, 1, i))
        go(a_hop(1, 1, i))
    b_side(0, 0).wait_recv()
    go(b_side(2, 0))

    def attend(rx, ry):
        s = slot(rx, ry)
        block = at_y(ry) * NX + at_x(rx)
        p = bp[sec * (NX * NY) + block]
        valid = plen[p] - seq * TILE
        scores = jnp.dot(kv[p, :, 0:HD], q[s], preferred_element_type=F32) * SCALE
        place = lax.broadcasted_iota(jnp.int32, (TILE, LANES), 0)
        scores = jnp.where(place < valid, scores, NEG)
        peak = jnp.max(scores, axis=0, keepdims=True)
        shift = jnp.where(valid > 0, peak, 0.0)
        weights = jnp.exp2(scores - shift).astype(BF16)
        own[s] = jnp.dot(vt[p], weights, preferred_element_type=F32)
        own[s, HD + 8 : PAY] = jnp.broadcast_to(peak, (8, LANES))

    for k in range(1, 6):
        if k <= 4:
            b_hop(0, k).wait_recv()
            if k < 4:
                go(b_hop(0, k + 1))
            go(b_side(0, -k))
            go(b_side(1, -k))
        if k <= 3:
            b_hop(1, k).wait_recv()
            if k < 3:
                go(b_hop(1, k + 1))
            go(b_side(0, k))
            go(b_side(1, k))
        signs = (1,) if k in (1, 5) else (1, -1)

        def blocks(i, carry, k=k, signs=signs):
            if k <= 4:
                a_hop(0, k, i).wait_recv()
                if k < 4:
                    a_hop(0, k + 1, i).start()
            if k <= 3:
                a_hop(1, k, i).wait_recv()
                if k < 3:
                    a_hop(1, k + 1, i).start()
            rx = i + (i // 2) * (1 - 2 * lax.rem(i, 2))
            for sign in signs:
                ry = sign * (k - 1)

                @pl.when(rx == 1)
                def _():
                    b_side(1, ry).wait_recv()

                @pl.when(rx == 2)
                def _():
                    b_side(2, ry).wait_recv()

                attend(rx, ry)
            return carry

        lax.fori_loop(0, NX, blocks, 0)
        if k <= 4:
            b_side(0, -k).wait_recv()
            go(b_side(2, -k))
        if k <= 3:
            b_side(0, k).wait_recv()
            go(b_side(2, k))

    def part_of(ref, h):
        cols = pl.ds(h * HALF, HALF)
        return ref[0:HD, cols], ref[HD : HD + 1, cols], ref[HD + 8 : HD + 9, cols]

    def arrived(ref):
        st = ref[HD:PAY].astype(F32)
        total = st[0:1] + st[1:2] + st[2:3]
        peak = st[8:9] + st[9:10] + st[10:11]
        return ref[0:HD].astype(F32), total, peak

    def merge(*parts):
        peak = parts[0][2]
        for part in parts[1:]:
            peak = jnp.maximum(peak, part[2])
        sums, total = None, None
        for o, l, m in parts:
            scale = jnp.exp2(m - peak)
            sums = o * scale if sums is None else sums + o * scale
            total = l * scale if total is None else total + l * scale
        return sums, total, peak

    def put(ref, part):
        o, l, m = part
        ref[0:HD] = o.astype(BF16)
        row = lax.broadcasted_iota(jnp.int32, (PAY - HD, HALF), 0)
        v = jnp.where(row < 8, l, m)
        high = v.astype(BF16).astype(F32)
        rest = v - high
        mid = rest.astype(BF16).astype(F32)
        low = rest - mid
        sub = lax.rem(row, 8)
        ref[HD:PAY] = jnp.where(sub == 0, high, jnp.where(sub == 1, mid, low)).astype(BF16)

    def oa_hop(arm, k, i):
        sign = 1 if arm == 0 else -1
        return copy(
            send_a.at[slot(i, sign * k)],
            ra_y.at[arm, k - 1, i],
            oay_s.at[arm, k - 1, i],
            oay_r.at[arm, k - 1, i],
            yp if arm == 0 else ym,
        )

    def ob_hop(arm, k):
        sign = 1 if arm == 0 else -1
        return copy(
            send_b.at[slot(0, sign * k)],
            rb_y.at[arm, k - 1],
            oby_s.at[arm, k - 1],
            oby_r.at[arm, k - 1],
            yp if arm == 0 else ym,
        )

    def ob_side(n, ry):
        return copy(
            send_b.at[slot((2, 1, 3)[n], ry)],
            rb_x.at[n, ry % NY],
            obx_s.at[n, ry % NY],
            obx_r.at[n, ry % NY],
            xm if n == 2 else xp,
        )

    def oa_side(n):
        return copy(
            send_a.at[slot((2, 1, 3)[n], 0)],
            ra_x.at[n],
            oax_s.at[n],
            oax_r.at[n],
            xm if n == 2 else xp,
        )

    def side_first(ry):
        put(send_b.at[slot(2, ry)], part_of(own.at[slot(2, ry)], 1))
        go(ob_side(0, ry))
        put(send_b.at[slot(3, ry)], part_of(own.at[slot(3, ry)], 1))
        go(ob_side(2, ry))

    def side_second(ry):
        ob_side(0, ry).wait_recv()
        put(
            send_b.at[slot(1, ry)],
            merge(part_of(own.at[slot(1, ry)], 1), arrived(rb_x.at[0, ry % NY])),
        )
        go(ob_side(1, ry))

    def side_last(ry):
        ob_side(2, ry).wait_recv()
        ob_side(1, ry).wait_recv()
        parts = [
            part_of(own.at[slot(0, ry)], 1),
            arrived(rb_x.at[1, ry % NY]),
            arrived(rb_x.at[2, ry % NY]),
        ]
        k = abs(ry)
        arm = 0 if ry > 0 else 1
        if k < (4 if arm == 0 else 3):
            ob_hop(arm, k + 1).wait_recv()
            parts.append(arrived(rb_y.at[arm, k]))
        put(send_b.at[slot(0, ry)], merge(*parts))
        go(ob_hop(arm, k))

    side_first(4)
    side_first(3)
    side_first(-3)
    for k in range(4, 0, -1):
        if k < 4:
            for ry in (k + 1, -k - 1):
                if ry != -4:
                    side_last(ry)

        def back(i, carry, k=k):
            for arm in range(2):
                if arm == 1 and k == 4:
                    continue
                s = slot(i, k if arm == 0 else -k)
                part = part_of(own.at[s], 0)
                if k < 4 - arm:
                    oa_hop(arm, k + 1, i).wait_recv()
                    part = merge(part, arrived(ra_y.at[arm, k, i]))
                put(send_a.at[s], part)
                oa_hop(arm, k, i).start()
            return carry

        lax.fori_loop(0, NX, back, 0)
        for ry in (k, -k):
            if ry != -4:
                side_second(ry)
        for ry in (k - 2, 2 - k):
            if k >= 3:
                side_first(ry)
        if k == 2:
            side_first(0)

    side_last(1)
    side_last(-1)

    def a_here(i):
        oa_hop(0, 1, i).wait_recv()
        oa_hop(1, 1, i).wait_recv()
        return [
            part_of(own.at[slot(i, 0)], 0),
            arrived(ra_y.at[0, 0, i]),
            arrived(ra_y.at[1, 0, i]),
        ]

    put(send_a.at[slot(2, 0)], merge(*a_here(2)))
    go(oa_side(0))
    put(send_a.at[slot(3, 0)], merge(*a_here(3)))
    go(oa_side(2))
    side_second(0)
    a_one = a_here(1)
    oa_side(0).wait_recv()
    put(send_a.at[slot(1, 0)], merge(*a_one, arrived(ra_x.at[0])))
    go(oa_side(1))

    lane_i = lax.rem(lax.broadcasted_iota(jnp.int32, (1, HALF), 1), BL)
    kept = lane_i < rlen[sec * (NX * NY) + seq]

    def finish(h, parts):
        o, l, _ = merge(part_of(mine, h), *parts)
        rows = jnp.where(kept, o / l, 0.0).T
        out[0, :, 2 * h * HD : (2 * h + 1) * HD] = rows[0:BL].astype(BF16)
        out[0, :, (2 * h + 1) * HD : (2 * h + 2) * HD] = rows[BL : 2 * BL].astype(BF16)

    ob_side(2, 0).wait_recv()
    ob_side(1, 0).wait_recv()
    ob_hop(0, 1).wait_recv()
    ob_hop(1, 1).wait_recv()
    finish(
        1,
        [part_of(own.at[0], 1)]
        + [arrived(r) for r in (rb_x.at[1, 0], rb_x.at[2, 0], rb_y.at[0, 0], rb_y.at[1, 0])],
    )
    a_zero = a_here(0)
    oa_side(2).wait_recv()
    oa_side(1).wait_recv()
    finish(0, a_zero + [arrived(ra_x.at[1]), arrived(ra_x.at[2])])

    for done in drains:
        done()

    def rest(i, carry):
        for k in range(2, 5):
            a_hop(0, k, i).wait_send()
            if k < 4:
                a_hop(1, k, i).wait_send()
        for k in range(1, 5):
            oa_hop(0, k, i).wait_send()
            if k < 4:
                oa_hop(1, k, i).wait_send()
        return carry

    lax.fori_loop(0, NX, rest, 0)

    @pl.when(sec == 0)
    def _():
        hand.wait_send()


def shards(hidden, carried, weight, responses, prompts, prompt_lengths, response_lengths, block_prompts):
    any_space = pl.BlockSpec(memory_space=pl.ANY)
    scalars = pl.BlockSpec(memory_space=pltpu.SMEM)
    dma = pltpu.SemaphoreType.DMA
    vmem = pltpu.VMEM
    sems = [
        (4,),
        None,
        None,
        (3,),
        (3,),
        (2, 4, 2),
        (2, 4, 2),
        (3,),
        (3,),
        (2, 4, NX),
        (2, 4, NX),
        (3,),
        (3,),
        (2, 4),
        (2, 4),
        (3, NY),
        (3, NY),
        (2, 4, NX),
        (2, 4, NX),
        (3,),
        (3,),
        (2, 4),
        (2, 4),
        (3, NY),
        (3, NY),
    ]
    return pl.pallas_call(
        kernel,
        out_shape=jax.ShapeDtypeStruct((1, BL, COLS), BF16),
        in_specs=[scalars] * 3 + [any_space] * 5,
        out_specs=pl.BlockSpec(memory_space=pltpu.VMEM),
        scratch_shapes=[
            vmem((BL, 4 * WIDE), BF16),
            vmem((BL, 4 * WIDE), BF16),
            vmem((NX, BL, WIDE), BF16),
            vmem((NX, BL, WIDE), BF16),
            vmem((NY, DEPTH, COLS), BF16),
            vmem((NX, BL, COLS), F32),
            vmem((3, BL, COLS), F32),
            vmem((NP, TILE, 2 * HD), BF16),
            vmem((BL, 2 * HD), BF16),
            vmem((NP, PAY, TILE), BF16),
            vmem((NX * NY, HD, LANES), BF16),
            vmem((NX * NY, PAY, LANES), F32),
            vmem((PAY, LANES), F32),
            vmem((NX * NY, PAY, HALF), BF16),
            vmem((NX * NY, PAY, HALF), BF16),
            vmem((2, 4, NX, PAY, HALF), BF16),
            vmem((3, PAY, HALF), BF16),
            vmem((2, 4, PAY, HALF), BF16),
            vmem((3, NY, PAY, HALF), BF16),
        ]
        + [dma if s is None else dma(s) for s in sems],
        compiler_params=pltpu.CompilerParams(
            collective_id=0, has_side_effects=True, vmem_limit_bytes=48 << 20
        ),
    )(
        block_prompts.reshape(-1),
        prompt_lengths,
        response_lengths.reshape(-1),
        hidden,
        carried,
        weight,
        responses,
        prompts,
    )


def solution(mesh):
    placed = (
        P("sec", "seq", None),
        P("sec", "seq", None),
        P("sec", "seq", "tp"),
        P("sec", "seq", "tp"),
        P("sec", None, "seq", "tp"),
        P(),
        P(),
        P(),
    )
    return jax.shard_map(
        shards, mesh=mesh, in_specs=placed, out_specs=P("sec", "seq", "tp"), check_vma=False
    )
```

time: 389 us -> 99.9 us (0.26)
  waiting for transfers between devices: 269 us -> 0 us
  Pallas kernels: 0 us -> 88.9 us
  local copies, waits for them, and re-layouts: 36.3 us -> 8.08 us
  matrix products: 26.7 us -> 0 us
  starting transfers between devices: 15.7 us -> 0 us
  between operations: 13.6 us -> 0.02 us
  blocking collectives: 12.8 us -> 0 us
  other arithmetic: 12.3 us -> 1.34 us
    all_gather x2 -> x0, waiting for transfers between devices: 174 us -> none  [the longest x1 92.6 us: shards(): lax.all_gather(query_weight[0], 'seq', axis=0, tiled=True)]
    all_to_all x2 -> x0, waiting for transfers between devices: 92.1 us -> none  [the longest x1 84 us: shards(): lax.all_to_all(sums, 'seq', split_axis=0, concat_axis=0, tiled=True)]
    pallas_call x0 -> x1, Pallas kernels: none -> 88.9 us  [shards(): pl.pallas_call(kernel, out_shape=jax.ShapeDtypeStruct((1, BL, COLS), BF16...]
    gather x32 -> x0, local copies, waits for them, and re-layouts: 32.4 us -> none  [the longest x24 27.3 us: tile_parts(): jnp.take(prompt_tiles, group_prompts, axis=0)]
    dot_general x19 -> x0, matrix products: 26.7 us -> none  [the longest x9 12 us: partial_attend(): jnp.einsum('rgqd,kgd->rgqk', queries, key_rows, preferred_element_type=jn...]
    all_to_all x2 -> x0, starting transfers between devices: 13.9 us -> none  [the longest x1 7.4 us: shards(): lax.all_to_all(peaks, 'seq', split_axis=0, concat_axis=0, tiled=True)]
    all_to_all x1 -> x0, blocking collectives: 12.8 us -> none  [shards(): lax.all_to_all(totals, 'seq', split_axis=0, concat_axis=0, tiled=True)]
    reduce_sum x11 -> x0, other arithmetic: 7.96 us -> none  [the longest x9 5.05 us: partial_attend(): row_total = jnp.sum(weights.astype(jnp.float32), axis=-1)]
  transfers between devices with their start and end apart: 5 -> 0, of which waited for: 5 -> 0; matrix products, arithmetic and copies ran while one was open for 1% -> 0% of each run, Pallas kernels for 0% -> 0%
where the time goes in v1:
time: 99.9 us; the launch traced here: 98.4 us
  Pallas kernels  88.9 us (89%)
  local copies, waits for them, and re-layouts  8.08 us (8%)
  other arithmetic  1.34 us (1%)
    pallas_call x1, Pallas kernels, shards(): pl.pallas_call(kernel, out_shape=jax.ShapeDtypeStruct((1, BL, COLS), BF16...  88.9 us
    unnamed x14, local copies, waits for them, and re-layouts  7.23 us

profile of v1, /device:TPU:6, one launch (start us, length us, event | category | flops | bytes accessed | tf_op | source)
XLA Modules:
  0.0 98.4 jit_solution(345554674459691712)
XLA Ops:
  0.0 0.8 reshape.7.rlen
  0.8 0.5 broadcast.3
  1.3 1.3 %reduce.3 = s32[2,32]{1,0:T(2,128)S(1)} reduce(s32[2,32,1]{1,2,0:T(1,128)} %param.15, s32[]{:T(128)} %broadcast.3), dimensions={2}, to_apply=%param.15.reduce_sub_computation.3 | reduce | bytes 516 | tf_op args[7]
  2.6 0.1 reshape.6.bp
  2.7 0.0 copy-start
  2.7 1.6 %copy-done = bf16[1,8,512,256]{3,2,1,0:T(8,128)(2,1)S(1)} copy-done((bf16[1,8,512,256]{3,2,1,0:T(8,128)(2,1)S(1)}, bf16[1,8,512,256]{3,2,1,0:T(8,128)(2,1)}, u32[]{:S(2)}) %copy-start) | copy-done | bytes 2097176
  4.3 0.0 copy-start.1
  4.3 1.1 %copy-done.1 = bf16[1,64,5120]{2,1,0:T(8,128)(2,1)S(1)} copy-done((bf16[1,64,5120]{2,1,0:T(8,128)(2,1)S(1)}, bf16[1,64,5120]{2,1,0:T(8,128)(2,1)}, u32[]{:S(2)}) %copy-start.1) | copy-done | bytes 655384
  5.4 0.0 copy-start.2
  5.4 1.1 %copy-done.2 = bf16[1,64,5120]{2,1,0:T(8,128)(2,1)S(1)} copy-done((bf16[1,64,5120]{2,1,0:T(8,128)(2,1)S(1)}, bf16[1,64,5120]{2,1,0:T(8,128)(2,1)}, u32[]{:S(2)}) %copy-start.2) | copy-done | bytes 655384
  6.5 0.0 copy-start.3
  6.5 0.9 copy-done.3
  7.4 0.0 copy-start.4
  7.4 0.8 copy-done.4
  8.1 0.0 copy-start.5
  8.1 0.7 copy-done.5
  8.8 88.9 %shard_map.82 = bf16[1,64,512]{2,1,0:T(8,128)(2,1)S(1)} custom-call(s32[64]{0:T(128)S(1)} %reshape.6.bp, s32[8]{0:T(128)S(1)} %copy-done.5, s32[64]{0:T(128)S(1)} %reshape.7.rlen, bf16[1,64,5120]{2,1,0:T(8,128)(2,1)S(1)} %copy-done.1, bf16[1,64,5120]{2,1,0:T(8,128)(2,1)S(1)} %copy-done.2, bf16[1,160,512]{2,1,0:T(8,128)(2,1)S(1)} %copy-done.3, ...), custom_call_target="tpu_custom_call" | custom-call | tf_op jit(solution)/shard_map/pallas_call | solution.py:604
  97.7 0.6 copy.10
Async XLA Ops:
  2.7 1.6 %copy-start = (bf16[1,8,512,256]{3,2,1,0:T(8,128)(2,1)S(1)}, bf16[1,8,512,256]{3,2,1,0:T(8,128)(2,1)}, u32[]{:S(2)}) copy-start(bf16[1,8,512,256]{3,2,1,0:T(8,128)(2,1)} %kv_h.1) | copy-start | bytes 6291460
  4.3 1.1 %copy-start.1 = (bf16[1,64,5120]{2,1,0:T(8,128)(2,1)S(1)}, bf16[1,64,5120]{2,1,0:T(8,128)(2,1)}, u32[]{:S(2)}) copy-start(bf16[1,64,5120]{2,1,0:T(8,128)(2,1)} %hid_h.1) | copy-start | bytes 1966084
  5.4 1.1 %copy-start.2 = (bf16[1,64,5120]{2,1,0:T(8,128)(2,1)S(1)}, bf16[1,64,5120]{2,1,0:T(8,128)(2,1)}, u32[]{:S(2)}) copy-start(bf16[1,64,5120]{2,1,0:T(8,128)(2,1)} %car_h.1) | copy-start | bytes 1966084
  6.5 0.9 copy-start.3
  7.4 0.8 copy-start.4
  8.1 0.7 copy-start.5

commit v2 on v0

v2 whole, which is shorter than its diff:
```python
import jax
import jax.numpy as jnp
from jax import lax
from jax.experimental import pallas as pl
from jax.experimental.pallas import tpu as pltpu
from jax.sharding import PartitionSpec as P

MESH = pl.DeviceIdType.MESH
HD = 128
NP = 8
TILE = 512
NX, NY = 4, 8
BL = 64
DEPTH = 160
WIDE = DEPTH * NY
COLS = 512
LANES = 256
HALF = 128
PAY = 144
SUB = DEPTH // 2
NEG = -1e30
SCALE = HD**-0.5 * 1.4426950408889634
F32 = jnp.float32
BF16 = jnp.bfloat16


def slot(rx, ry):
    return lax.rem(ry + NY, NY) * NX + rx if not isinstance(ry, int) else (ry % NY) * NX + rx


def kernel(
    bp,
    plen,
    rlen,
    hid_h,
    car_h,
    w_h,
    rc_h,
    kv_h,
    out,
    hid,
    handed,
    xin,
    lhs,
    transit,
    wbuf,
    pbuf,
    prec,
    kv,
    rc,
    vt,
    q,
    own,
    mine,
    back,
    from_y,
    from_x,
    local_sem,
    hand_s,
    hand_r,
    xin_s,
    xin_r,
    w_s,
    w_r,
    p_s,
    p_r,
    qy_s,
    qy_r,
    qx_s,
    qx_r,
    oy_s,
    oy_r,
    ox_s,
    ox_r,
):
    sec = lax.axis_index("sec")
    seq = lax.axis_index("seq")
    y, x = seq // NX, lax.rem(seq, NX)
    turn = 1 - 2 * sec

    def at_x(rx):
        return lax.rem(x + turn * rx + 2 * NX, NX)

    def at_y(ry):
        return lax.rem(y + turn * ry + 2 * NY, NY)

    def dev(rx, ry):
        return at_y(ry) * NX + at_x(rx)

    xp, xm, x2 = dev(1, 0), dev(-1, 0), dev(2, 0)
    yp, ym = dev(0, 1), dev(0, -1)
    drains = []

    def copy(src, dst, ss, rs, where):
        return pltpu.make_async_remote_copy(
            src_ref=src,
            dst_ref=dst,
            send_sem=ss,
            recv_sem=rs,
            device_id={"seq": where},
            device_id_type=MESH,
        )

    def push(src, dst, ss, rs, where):
        c = copy(src, dst, ss, rs, where)
        c.start()
        drains.append(c.wait_send)

    def got(dst, rs):
        copy(dst, dst, rs, rs, xp).wait_recv()

    in_hid = pltpu.make_async_copy(hid_h.at[0], hid, local_sem.at[0])
    in_kv = pltpu.make_async_copy(kv_h.at[0], kv, local_sem.at[1])
    in_rc = pltpu.make_async_copy(rc_h.at[0], rc, local_sem.at[2])
    in_w = pltpu.make_async_copy(w_h.at[0], wbuf.at[y], local_sem.at[3])
    in_hid.start()
    in_w.start()
    in_kv.start()
    in_rc.start()

    barrier = pltpu.get_barrier_semaphore()
    for where in (xp, xm, x2, yp, ym):
        pl.semaphore_signal(barrier, inc=1, device_id={"seq": where}, device_id_type=MESH)

    @pl.when(sec == 1)
    def _():
        pl.semaphore_signal(barrier, inc=1, device_id={"sec": 0}, device_id_type=MESH)
        pl.semaphore_wait(barrier, 5)

    @pl.when(sec == 0)
    def _():
        pl.semaphore_wait(barrier, 6)

    hand = pltpu.make_async_remote_copy(
        src_ref=car_h.at[0],
        dst_ref=handed,
        send_sem=hand_s,
        recv_sem=hand_r,
        device_id={"sec": 1},
        device_id_type=MESH,
    )

    @pl.when(sec == 0)
    def _():
        hand.start()

    wide = COLS // 2

    def w_part(ry, h, r):
        return wbuf.at[at_y(ry), pl.ds(r * SUB, SUB), pl.ds(h * wide, wide)]

    def w_hop(arm, k, h, r):
        sign = -1 if arm == 0 else 1
        part = w_part(sign * (k - 1), h, r)
        src = w_h.at[0, pl.ds(r * SUB, SUB), pl.ds(h * wide, wide)] if k == 1 else part
        where = yp if arm == 0 else ym
        return copy(src, part, w_s.at[arm, k - 1, h, r], w_r.at[arm, k - 1, h, r], where)

    def go(c):
        c.start()
        drains.append(c.wait_send)

    def w_on(k, h):
        for r in range(2):
            for arm in range(2):
                if k <= 4 - arm:
                    if k > 0:
                        got(w_part((-k, k)[arm], h, r), w_r.at[arm, k - 1, h, r])
                    if k < 4 - arm:
                        go(w_hop(arm, k + 1, h, r))

    w_on(0, 0)
    w_on(0, 1)

    rows_of = [pl.ds(r * (BL // 2), BL // 2) for r in range(2)]
    far_out = [
        copy(xin.at[at_x(2), rows], transit.at[rows], xin_s.at[2, r], xin_r.at[2, r], xp)
        for r, rows in enumerate(rows_of)
    ]
    far_on = [
        copy(transit.at[rows], lhs.at[2, rows], xin_s.at[3, r], xin_r.at[3, r], xp)
        for r, rows in enumerate(rows_of)
    ]
    near_out = [
        copy(xin.at[at_x(-1)], lhs.at[1], xin_s.at[1, 0], xin_r.at[1, 0], xm),
        copy(xin.at[at_x(1)], lhs.at[3], xin_s.at[0, 0], xin_r.at[0, 0], xp),
    ]

    def regroup(with_handed):
        def rows16(r, carry):
            rows = pl.ds(pl.multiple_of(r * 16, 16), 16)
            lane = lax.broadcasted_iota(jnp.int32, (16, 4 * DEPTH), 1)
            for g in range(2):
                parts = []
                for j in range(4):
                    cols = pl.ds(4 * DEPTH * (4 * g + j), 4 * DEPTH)
                    v = hid[rows, cols].astype(F32)
                    if with_handed:
                        v = v + handed[rows, cols].astype(F32)
                        v = v.astype(BF16).astype(F32)
                    parts.append(v)
                for xx in range(NX):
                    total = None
                    for j in range(4):
                        shift = (DEPTH * (j - xx)) % (4 * DEPTH)
                        v = parts[j] if shift == 0 else pltpu.roll(parts[j], shift, 1)
                        total = v if total is None else jnp.where(lane >= DEPTH * j, v, total)
                    xin[xx, rows, pl.ds(4 * DEPTH * g, 4 * DEPTH)] = total.astype(BF16)
            return carry

        lax.fori_loop(0, BL // 16, rows16, 0)

    def values_across(p, carry):
        vt[p, 0:HD, :] = kv[p, :, HD : 2 * HD].astype(F32).T.astype(BF16)
        vt[p, HD:PAY, :] = jnp.ones((PAY - HD, TILE), BF16)
        return carry

    in_hid.wait()

    @pl.when(sec == 0)
    def _():
        regroup(False)

    @pl.when(sec == 1)
    def _():
        hand.wait_recv()
        regroup(True)

    for c in (*far_out, *near_out):
        go(c)
    lhs[0] = xin[x]
    w_on(1, 0)
    w_on(2, 0)
    w_on(1, 1)
    for come, on_c in zip(far_out, far_on):
        come.wait_recv()
        go(on_c)
    in_kv.wait()
    lax.fori_loop(0, 3, values_across, 0)
    w_on(3, 0)
    w_on(2, 1)
    lax.fori_loop(3, 5, values_across, 0)
    w_on(4, 0)

    in_w.wait()
    in_rc.wait()
    for c in (*near_out, *far_on):
        c.wait_recv()

    def heads(ref, n, h):
        return ref.at[n, :, pl.ds(h * wide, wide)]

    def partial(first, h):
        rows = jnp.dot(
            lhs[first : first + 2].reshape(2 * BL, WIDE),
            wbuf[:, :, h * wide : (h + 1) * wide].reshape(WIDE, wide),
            preferred_element_type=F32,
        )
        pbuf[first : first + 2, :, h * wide : (h + 1) * wide] = rows.reshape(2, BL, wide)

    def send_partial(src, dst, h, where):
        push(heads(pbuf, src, h), heads(prec, dst, h), p_s.at[dst, h], p_r.at[dst, h], where)

    def partials(h):
        partial(2, h)
        send_partial(2, 0, h, xp)
        send_partial(3, 2, h, xm)
        partial(0, h)

    def add_far(h):
        cols = slice(h * wide, (h + 1) * wide)
        got(heads(prec, 0, h), p_r.at[0, h])
        pbuf[1, :, cols] = pbuf[1, :, cols] + prec[0, :, cols]
        send_partial(1, 1, h, xp)

    def my_queries(h):
        cols = slice(h * wide, (h + 1) * wide)
        got(heads(prec, 2, h), p_r.at[2, h])
        got(heads(prec, 1, h), p_r.at[1, h])
        mine_q = pbuf[0, :, cols] + prec[1, :, cols] + prec[2, :, cols]
        both = jnp.concatenate([mine_q[:, 0:HD], mine_q[:, HD : 2 * HD]], axis=0)
        q[0, :, h * HALF : (h + 1) * HALF] = both.T.astype(BF16)

    def half(s, h):
        return q.at[s, :, pl.ds(h * HALF, HALF)]

    def y_out(arm, k, h, i):
        sign = -1 if arm == 0 else 1
        return copy(
            half(slot(i, sign * (k - 1)), h),
            half(slot(i, sign * k), h),
            qy_s.at[arm, k - 1, h, i],
            qy_r.at[arm, k - 1, h, i],
            yp if arm == 0 else ym,
        )

    x_side = [
        [
            copy(half(0, h), half(dst, h), qx_s.at[dst - 1, h], qx_r.at[dst - 1, h], where)
            for dst, where in ((1, xm), (3, xp), (2, x2))
        ]
        for h in range(2)
    ]

    def on(k, h, *columns):
        for i in columns or (0, 1, 3, 2):
            for arm in range(2):
                if k <= 4 - arm:
                    if k > 0:
                        y_out(arm, k, h, i).wait_recv()
                    if k < 4 - arm:
                        go(y_out(arm, k + 1, h, i))

    def row_of(h):
        my_queries(h)
        for c in x_side[h]:
            go(c)
        on(0, h, 0)

    def row_on(h):
        for c, i in zip(x_side[h], (1, 3, 2)):
            c.wait_recv()
            on(0, h, i)

    def attend(ry):
        spots = [slot(rx, ry) for rx in range(NX)]
        prompts = [bp[sec, 0, at_y(ry) * NX + at_x(rx)] for rx in range(NX)]
        valid = [plen[p] - seq * TILE for p in prompts]
        place = lax.broadcasted_iota(jnp.int32, (TILE, LANES), 0)
        scores = []
        for s, p, v in zip(spots, prompts, valid):
            raw = jnp.dot(kv[p, :, 0:HD], q[s], preferred_element_type=F32)
            scores.append(jnp.where(place < v, raw * SCALE, NEG))
        weights = []
        for s, v, score in zip(spots, valid, scores):
            peak = jnp.max(score, axis=0, keepdims=True)
            shift = jnp.where(v > 0, peak, 0.0)
            weights.append((peak, jnp.exp2(score - shift).astype(BF16)))
        for s, p, (peak, w) in zip(spots, prompts, weights):
            own[s] = jnp.dot(vt[p], w, preferred_element_type=F32)
            own[s, HD + 8 : PAY] = jnp.broadcast_to(peak, (8, LANES))

    partials(0)
    w_on(3, 1)
    add_far(0)
    lax.fori_loop(5, NP, values_across, 0)
    w_on(4, 1)
    partials(1)
    row_of(0)
    add_far(1)
    row_on(0)
    row_of(1)
    on(1, 0)

    own_s = jnp.dot(rc[:, 0:HD], q[0], preferred_element_type=F32) * SCALE
    own_t = lax.broadcasted_iota(jnp.int32, (BL, LANES), 0)
    own_i = lax.rem(lax.broadcasted_iota(jnp.int32, (BL, LANES), 1), BL)
    own_s = jnp.where(own_t <= own_i, own_s, NEG)
    own_m = jnp.max(own_s, axis=0, keepdims=True)
    own_w = jnp.exp2(own_s - own_m).astype(BF16)
    own_v = rc[:, HD : 2 * HD].astype(F32).T.astype(BF16)
    mine[0:HD] = jnp.dot(own_v, own_w, preferred_element_type=F32)
    mine[HD : HD + 8] = jnp.broadcast_to(
        jnp.sum(own_w.astype(F32), axis=0, keepdims=True), (8, LANES)
    )
    mine[HD + 8 : PAY] = jnp.broadcast_to(own_m, (8, LANES))

    def widths(ry):
        return (slice(0, HALF), slice(HALF, LANES)) if abs(ry) > 2 else (slice(0, LANES),)

    def part_of(ref, cols):
        return ref[0:HD, cols], ref[HD : HD + 1, cols], ref[HD + 8 : HD + 9, cols]

    def arrived(ref, cols):
        st = ref[HD:PAY, cols].astype(F32)
        total = st[0:1] + st[1:2] + st[2:3]
        peak = st[8:9] + st[9:10] + st[10:11]
        return ref[0:HD, cols].astype(F32), total, peak

    def merge(*parts):
        peak = parts[0][2]
        for part in parts[1:]:
            peak = jnp.maximum(peak, part[2])
        sums, total = None, None
        for o, l, m in parts:
            scale = jnp.exp2(m - peak)
            sums = o * scale if sums is None else sums + o * scale
            total = l * scale if total is None else total + l * scale
        return sums, total, peak

    def put(s, cols, part):
        o, l, m = part
        back[s, 0:HD, cols] = o.astype(BF16)
        row = lax.broadcasted_iota(jnp.int32, (PAY - HD, o.shape[1]), 0)
        v = jnp.where(row < 8, l, m)
        high = v.astype(BF16).astype(F32)
        rest = v - high
        mid = rest.astype(BF16).astype(F32)
        low = rest - mid
        sub = lax.rem(row, 8)
        three = jnp.where(sub == 0, high, jnp.where(sub == 1, mid, low))
        back[s, HD:PAY, cols] = three.astype(BF16)

    def lanes_of(cols):
        return pl.ds(cols.start, cols.stop - cols.start)

    def x_hop(n, ry, w):
        lanes = lanes_of(widths(ry)[w])
        return copy(
            back.at[slot((2, 1, 3)[n], ry), :, lanes],
            from_x.at[n, ry % NY, :, lanes],
            ox_s.at[n, ry % NY, w],
            ox_r.at[n, ry % NY, w],
            xm if n == 2 else xp,
        )

    def y_hop(arm, k, w):
        lanes = pl.ds(w * HALF, HALF)
        return copy(
            back.at[slot(0, (k, -k)[arm]), :, lanes],
            from_y.at[arm, k - 1, :, lanes],
            oy_s.at[arm, k - 1, w],
            oy_r.at[arm, k - 1, w],
            yp if arm == 0 else ym,
        )

    def first(ry):
        for w, cols in enumerate(widths(ry)):
            for rx, n in ((2, 0), (3, 2)):
                put(slot(rx, ry), cols, part_of(own.at[slot(rx, ry)], cols))
                go(x_hop(n, ry, w))

    def second(ry):
        for w, cols in enumerate(widths(ry)):
            x_hop(0, ry, w).wait_recv()
            s = slot(1, ry)
            put(s, cols, merge(part_of(own.at[s], cols), arrived(from_x.at[0, ry % NY], cols)))
            go(x_hop(1, ry, w))

    def joined(ry, w, cols):
        x_hop(2, ry, w).wait_recv()
        x_hop(1, ry, w).wait_recv()
        return merge(
            part_of(own.at[slot(0, ry)], cols),
            arrived(from_x.at[2, ry % NY], cols),
            arrived(from_x.at[1, ry % NY], cols),
        )

    def join(ry):
        for w, cols in enumerate(widths(ry)):
            o, l, m = joined(ry, w, cols)
            s = slot(0, ry)
            own[s, 0:HD, cols] = o
            own[s, HD : HD + 8, cols] = jnp.broadcast_to(l, (8, l.shape[1]))
            own[s, HD + 8 : PAY, cols] = jnp.broadcast_to(m, (8, m.shape[1]))

    def home(ry):
        arm, k, s = int(ry < 0), abs(ry), slot(0, ry)
        for w in range(2):
            cols = slice(w * HALF, (w + 1) * HALF)
            if k == 4 - arm:
                part = joined(ry, w, cols)
            else:
                y_hop(arm, k + 1, w).wait_recv()
                part = merge(part_of(own.at[s], cols), arrived(from_y.at[arm, k], cols))
            put(s, cols, part)
            go(y_hop(arm, k, w))

    row_on(1)
    on(2, 0)
    on(1, 1, 0, 1)
    attend(0)
    first(0)
    on(1, 1, 3, 2)
    on(3, 0, 0, 1)
    attend(1)
    first(1)
    on(3, 0, 3, 2)
    second(0)
    on(2, 1, 0, 1)
    attend(-1)
    first(-1)
    on(2, 1, 3, 2)
    second(1)
    attend(2)
    first(2)
    on(3, 1, 0, 1)
    second(-1)
    attend(-2)
    first(-2)
    on(3, 1, 3, 2)
    second(2)
    attend(-3)
    first(-3)
    second(-2)
    attend(3)
    first(3)
    on(4, 0)
    on(4, 1)
    attend(4)
    first(4)
    second(-3)
    second(3)
    join(0)
    join(1)
    second(4)
    home(-3)
    join(-1)
    join(3)
    join(2)
    join(-2)
    home(4)
    home(-2)
    home(3)
    home(-1)
    home(2)
    home(1)

    lane_i = lax.rem(lax.broadcasted_iota(jnp.int32, (1, HALF), 1), BL)
    kept = lane_i < rlen[sec, seq]

    for h in range(2):
        cols = slice(h * HALF, (h + 1) * HALF)
        y_hop(1, 1, h).wait_recv()
        y_hop(0, 1, h).wait_recv()
        o, l, _ = merge(
            part_of(mine, cols),
            part_of(own.at[0], cols),
            arrived(from_y.at[1, 0], cols),
            arrived(from_y.at[0, 0], cols),
        )
        rows = jnp.where(kept, o / l, 0.0).T
        out[0, :, 2 * h * HD : (2 * h + 1) * HD] = rows[0:BL].astype(BF16)
        out[0, :, (2 * h + 1) * HD : (2 * h + 2) * HD] = rows[BL : 2 * BL].astype(BF16)

    for done in drains:
        done()

    @pl.when(sec == 0)
    def _():
        hand.wait_send()


def shards(hidden, carried, weight, responses, prompts, prompt_lengths, response_lengths, block_prompts):
    any_space = pl.BlockSpec(memory_space=pltpu.HBM)
    scalars = pl.BlockSpec(memory_space=pltpu.SMEM)
    dma = pltpu.SemaphoreType.DMA
    vmem = pltpu.VMEM
    sems = [
        (4,),
        None,
        None,
        (4, 2),
        (4, 2),
        (2, 4, 2, 2),
        (2, 4, 2, 2),
        (3, 2),
        (3, 2),
        (2, 4, 2, NX),
        (2, 4, 2, NX),
        (3, 2),
        (3, 2),
        (2, 4, 2),
        (2, 4, 2),
        (3, NY, 2),
        (3, NY, 2),
    ]
    return pl.pallas_call(
        kernel,
        out_shape=jax.ShapeDtypeStruct((1, BL, COLS), BF16),
        in_specs=[scalars] * 3 + [any_space] * 5,
        out_specs=pl.BlockSpec(memory_space=pltpu.VMEM),
        scratch_shapes=[
            vmem((BL, 4 * WIDE), BF16),
            vmem((BL, 4 * WIDE), BF16),
            vmem((NX, BL, WIDE), BF16),
            vmem((NX, BL, WIDE), BF16),
            vmem((BL, WIDE), BF16),
            vmem((NY, DEPTH, COLS), BF16),
            vmem((NX, BL, COLS), F32),
            vmem((3, BL, COLS), F32),
            vmem((NP, TILE, 2 * HD), BF16),
            vmem((BL, 2 * HD), BF16),
            vmem((NP, PAY, TILE), BF16),
            vmem((NX * NY, HD, LANES), BF16),
            vmem((NX * NY, PAY, LANES), F32),
            vmem((PAY, LANES), F32),
            vmem((NX * NY, PAY, LANES), BF16),
            vmem((2, 4, PAY, LANES), BF16),
            vmem((3, NY, PAY, LANES), BF16),
        ]
        + [dma if s is None else dma(s) for s in sems],
        compiler_params=pltpu.CompilerParams(
            collective_id=0, has_side_effects=True, vmem_limit_bytes=63 << 20
        ),
    )(
        jnp.swapaxes(block_prompts, 1, 2),
        prompt_lengths,
        response_lengths,
        hidden,
        carried,
        weight,
        responses,
        prompts,
    )


def solution(mesh):
    placed = (
        P("sec", "seq", None),
        P("sec", "seq", None),
        P("sec", "seq", "tp"),
        P("sec", "seq", "tp"),
        P("sec", None, "seq", "tp"),
        P(),
        P(),
        P(),
    )
    return jax.shard_map(
        shards, mesh=mesh, in_specs=placed, out_specs=P("sec", "seq", "tp"), check_vma=False
    )
```

time: 389 us -> 85.1 us (0.22)
  waiting for transfers between devices: 269 us -> 0 us
  Pallas kernels: 0 us -> 82.4 us
  local copies, waits for them, and re-layouts: 36.3 us -> 1.47 us
  matrix products: 26.7 us -> 0 us
  starting transfers between devices: 15.7 us -> 0 us
  between operations: 13.6 us -> 0.01 us
  blocking collectives: 12.8 us -> 0 us
  other arithmetic: 12.3 us -> 0 us
    all_gather x2 -> x0, waiting for transfers between devices: 174 us -> none  [the longest x1 92.6 us: shards(): lax.all_gather(query_weight[0], 'seq', axis=0, tiled=True)]
    all_to_all x2 -> x0, waiting for transfers between devices: 92.1 us -> none  [the longest x1 84 us: shards(): lax.all_to_all(sums, 'seq', split_axis=0, concat_axis=0, tiled=True)]
    pallas_call x0 -> x1, Pallas kernels: none -> 82.4 us  [shards(): pl.pallas_call(kernel, out_shape=jax.ShapeDtypeStruct((1, BL, COLS), BF16...]
    gather x32 -> x0, local copies, waits for them, and re-layouts: 32.4 us -> none  [the longest x24 27.3 us: tile_parts(): jnp.take(prompt_tiles, group_prompts, axis=0)]
    dot_general x19 -> x0, matrix products: 26.7 us -> none  [the longest x9 12 us: partial_attend(): jnp.einsum('rgqd,kgd->rgqk', queries, key_rows, preferred_element_type=jn...]
    all_to_all x2 -> x0, starting transfers between devices: 13.9 us -> none  [the longest x1 7.4 us: shards(): lax.all_to_all(peaks, 'seq', split_axis=0, concat_axis=0, tiled=True)]
    all_to_all x1 -> x0, blocking collectives: 12.8 us -> none  [shards(): lax.all_to_all(totals, 'seq', split_axis=0, concat_axis=0, tiled=True)]
    reduce_sum x11 -> x0, other arithmetic: 7.96 us -> none  [the longest x9 5.05 us: partial_attend(): row_total = jnp.sum(weights.astype(jnp.float32), axis=-1)]
  transfers between devices with their start and end apart: 5 -> 0, of which waited for: 5 -> 0; matrix products, arithmetic and copies ran while one was open for 1% -> 0% of each run, Pallas kernels for 0% -> 0%
where the time goes in v2:
time: 85.1 us; the launch traced here: 83.9 us
  Pallas kernels  82.4 us (97%)
  local copies, waits for them, and re-layouts  1.47 us (2%)
    pallas_call x1, Pallas kernels, shards(): pl.pallas_call(kernel, out_shape=jax.ShapeDtypeStruct((1, BL, COLS), BF16...  82.4 us

profile of v2, /device:TPU:6, one launch (start us, length us, event | category | flops | bytes accessed | tf_op | source)
XLA Modules:
  0.0 83.9 jit_solution(17408193214680945316)
XLA Ops:
  0.0 82.4 %shard_map.82 = bf16[1,64,512]{2,1,0:T(8,128)(2,1)} custom-call(s32[2,1,32]{2,1,0:T(1,128)} %bitcast.3, s32[8]{0:T(128)} %plen.1, s32[2,32]{1,0:T(2,128)} %rlen.1, bf16[1,64,5120]{2,1,0:T(8,128)(2,1)} %hid_h.1, bf16[1,64,5120]{2,1,0:T(8,128)(2,1)} %car_h.1, bf16[1,160,512]{2,1,0:T(8,128)(2,1)} %w_h.1, bf16[1,64,256]{2,1,0:T(8,128)(2,1)} %rc_h.1, ...), custom_call_target="tpu_custom_call" | custom-call | tf_op jit(solution)/shard_map/pallas_call | solution.py:568
  82.4 1.5 %copy.11 = bf16[1,64,512]{2,1,0:T(8,128)(2,1)} copy(bf16[1,64,512]{2,1,0:T(8,128)(2,1)} %shard_map.82) | data formatting | bytes 131072

commit v3 on v2

--- a/solution.py
+++ b/solution.py
@@ -29,15 +29,18 @@
 
 
 def kernel(
-    bp,
-    plen,
-    rlen,
+    bp_h,
+    plen_h,
+    rlen_h,
     hid_h,
     car_h,
     w_h,
     rc_h,
     kv_h,
     out,
+    bp,
+    plen,
+    rlen,
     hid,
     handed,
     xin,
@@ -88,7 +91,8 @@
         return at_y(ry) * NX + at_x(rx)
 
     xp, xm, x2 = dev(1, 0), dev(-1, 0), dev(2, 0)
-    yp, ym = dev(0, 1), dev(0, -1)
+    yp, ym, y4 = dev(0, 1), dev(0, -1), dev(0, 4)
+    y3 = (dev(0, 3), dev(0, -3))
     drains = []
 
     def copy(src, dst, ss, rs, where):
@@ -113,23 +117,29 @@
     in_kv = pltpu.make_async_copy(kv_h.at[0], kv, local_sem.at[1])
     in_rc = pltpu.make_async_copy(rc_h.at[0], rc, local_sem.at[2])
     in_w = pltpu.make_async_copy(w_h.at[0], wbuf.at[y], local_sem.at[3])
+    in_scalars = [
+        pltpu.make_async_copy(src, dst, local_sem.at[4 + n])
+        for n, (src, dst) in enumerate(((bp_h, bp), (plen_h, plen), (rlen_h, rlen)))
+    ]
     in_hid.start()
     in_w.start()
     in_kv.start()
     in_rc.start()
+    for c in in_scalars:
+        c.start()
 
     barrier = pltpu.get_barrier_semaphore()
-    for where in (xp, xm, x2, yp, ym):
+    for where in (xp, xm, x2, yp, ym, y4, *y3):
         pl.semaphore_signal(barrier, inc=1, device_id={"seq": where}, device_id_type=MESH)
 
     @pl.when(sec == 1)
     def _():
         pl.semaphore_signal(barrier, inc=1, device_id={"sec": 0}, device_id_type=MESH)
-        pl.semaphore_wait(barrier, 5)
+        pl.semaphore_wait(barrier, 8)
 
     @pl.when(sec == 0)
     def _():
-        pl.semaphore_wait(barrier, 6)
+        pl.semaphore_wait(barrier, 9)
 
     hand = pltpu.make_async_remote_copy(
         src_ref=car_h.at[0],
@@ -140,10 +150,6 @@
         device_id_type=MESH,
     )
 
-    @pl.when(sec == 0)
-    def _():
-        hand.start()
-
     wide = COLS // 2
 
     def w_part(ry, h, r):
@@ -171,6 +177,11 @@
 
     w_on(0, 0)
     w_on(0, 1)
+
+    @pl.when(sec == 0)
+    def _():
+        hand.start()
+
 
     rows_of = [pl.ds(r * (BL // 2), BL // 2) for r in range(2)]
     far_out = [
@@ -244,6 +255,8 @@
 
     in_w.wait()
     in_rc.wait()
+    for c in in_scalars:
+        c.wait()
     for c in (*near_out, *far_on):
         c.wait_recv()
 
@@ -263,21 +276,17 @@
 
     def partials(h):
         partial(2, h)
-        send_partial(2, 0, h, xp)
+        send_partial(2, 0, h, x2)
         send_partial(3, 2, h, xm)
         partial(0, h)
-
-    def add_far(h):
-        cols = slice(h * wide, (h + 1) * wide)
-        got(heads(prec, 0, h), p_r.at[0, h])
-        pbuf[1, :, cols] = pbuf[1, :, cols] + prec[0, :, cols]
         send_partial(1, 1, h, xp)
 
     def my_queries(h):
         cols = slice(h * wide, (h + 1) * wide)
         got(heads(prec, 2, h), p_r.at[2, h])
         got(heads(prec, 1, h), p_r.at[1, h])
-        mine_q = pbuf[0, :, cols] + prec[1, :, cols] + prec[2, :, cols]
+        got(heads(prec, 0, h), p_r.at[0, h])
+        mine_q = pbuf[0, :, cols] + prec[1, :, cols] + prec[2, :, cols] + prec[0, :, cols]
         both = jnp.concatenate([mine_q[:, 0:HD], mine_q[:, HD : 2 * HD]], axis=0)
         q[0, :, h * HALF : (h + 1) * HALF] = both.T.astype(BF16)
 
@@ -342,12 +351,10 @@
 
     partials(0)
     w_on(3, 1)
-    add_far(0)
     lax.fori_loop(5, NP, values_across, 0)
     w_on(4, 1)
     partials(1)
     row_of(0)
-    add_far(1)
     row_on(0)
     row_of(1)
     on(1, 0)
@@ -366,7 +373,7 @@
     mine[HD + 8 : PAY] = jnp.broadcast_to(own_m, (8, LANES))
 
     def widths(ry):
-        return (slice(0, HALF), slice(HALF, LANES)) if abs(ry) > 2 else (slice(0, LANES),)
+        return (slice(0, HALF), slice(HALF, LANES)) if abs(ry) > 1 else (slice(0, LANES),)
 
     def part_of(ref, cols):
         return ref[0:HD, cols], ref[HD : HD + 1, cols], ref[HD + 8 : HD + 9, cols]
@@ -411,7 +418,7 @@
             from_x.at[n, ry % NY, :, lanes],
             ox_s.at[n, ry % NY, w],
             ox_r.at[n, ry % NY, w],
-            xm if n == 2 else xp,
+            xm if n == 2 else x2 if n == 0 and abs(ry) > 2 else xp,
         )
 
     def y_hop(arm, k, w):
@@ -421,12 +428,12 @@
             from_y.at[arm, k - 1, :, lanes],
             oy_s.at[arm, k - 1, w],
             oy_r.at[arm, k - 1, w],
-            yp if arm == 0 else ym,
+            y4 if k == 4 else y3[arm] if k == 3 else (yp, ym)[arm],
         )
 
     def first(ry):
         for w, cols in enumerate(widths(ry)):
-            for rx, n in ((2, 0), (3, 2)):
+            for rx, n in ((2, 0), (3, 2), (1, 1))[: 3 if abs(ry) > 2 else 2]:
                 put(slot(rx, ry), cols, part_of(own.at[slot(rx, ry)], cols))
                 go(x_hop(n, ry, w))
 
@@ -438,12 +445,12 @@
             go(x_hop(1, ry, w))
 
     def joined(ry, w, cols):
-        x_hop(2, ry, w).wait_recv()
-        x_hop(1, ry, w).wait_recv()
+        hops = (2, 1, 0) if abs(ry) > 2 else (2, 1)
+        for n in hops:
+            x_hop(n, ry, w).wait_recv()
         return merge(
             part_of(own.at[slot(0, ry)], cols),
-            arrived(from_x.at[2, ry % NY], cols),
-            arrived(from_x.at[1, ry % NY], cols),
+            *[arrived(from_x.at[n, ry % NY], cols) for n in hops],
         )
 
     def join(ry):
@@ -458,7 +465,7 @@
         arm, k, s = int(ry < 0), abs(ry), slot(0, ry)
         for w in range(2):
             cols = slice(w * HALF, (w + 1) * HALF)
-            if k == 4 - arm:
+            if k >= 2:
                 part = joined(ry, w, cols)
             else:
                 y_hop(arm, k + 1, w).wait_recv()
@@ -499,21 +506,15 @@
     on(4, 1)
     attend(4)
     first(4)
-    second(-3)
-    second(3)
     join(0)
     join(1)
-    second(4)
     home(-3)
+    home(3)
+    home(-2)
+    home(2)
+    home(4)
     join(-1)
-    join(3)
-    join(2)
-    join(-2)
-    home(4)
-    home(-2)
-    home(3)
     home(-1)
-    home(2)
     home(1)
 
     lane_i = lax.rem(lax.broadcasted_iota(jnp.int32, (1, HALF), 1), BL)
@@ -523,11 +524,17 @@
         cols = slice(h * HALF, (h + 1) * HALF)
         y_hop(1, 1, h).wait_recv()
         y_hop(0, 1, h).wait_recv()
+        y_hop(0, 3, h).wait_recv()
+        y_hop(1, 3, h).wait_recv()
+        y_hop(0, 4, h).wait_recv()
         o, l, _ = merge(
             part_of(mine, cols),
             part_of(own.at[0], cols),
             arrived(from_y.at[1, 0], cols),
             arrived(from_y.at[0, 0], cols),
+            arrived(from_y.at[0, 2], cols),
+            arrived(from_y.at[1, 2], cols),
+            arrived(from_y.at[0, 3], cols),
         )
         rows = jnp.where(kept, o / l, 0.0).T
         out[0, :, 2 * h * HD : (2 * h + 1) * HD] = rows[0:BL].astype(BF16)
@@ -543,11 +550,10 @@
 
 def shards(hidden, carried, weight, responses, prompts, prompt_lengths, response_lengths, block_prompts):
     any_space = pl.BlockSpec(memory_space=pltpu.HBM)
-    scalars = pl.BlockSpec(memory_space=pltpu.SMEM)
     dma = pltpu.SemaphoreType.DMA
     vmem = pltpu.VMEM
     sems = [
-        (4,),
+        (7,),
         None,
         None,
         (4, 2),
@@ -568,9 +574,12 @@
     return pl.pallas_call(
         kernel,
         out_shape=jax.ShapeDtypeStruct((1, BL, COLS), BF16),
-        in_specs=[scalars] * 3 + [any_space] * 5,
+        in_specs=[any_space] * 8,
         out_specs=pl.BlockSpec(memory_space=pltpu.VMEM),
         scratch_shapes=[
+            pltpu.SMEM((2, 1, NX * NY), jnp.int32),
+            pltpu.SMEM((NP,), jnp.int32),
+            pltpu.SMEM((2, NX * NY), jnp.int32),
             vmem((BL, 4 * WIDE), BF16),
             vmem((BL, 4 * WIDE), BF16),
             vmem((NX, BL, WIDE), BF16),

time: 85.1 us -> 80.1 us (0.941)
  Pallas kernels: 82.4 us -> 78 us
    pallas_call x1, Pallas kernels: 82.4 us -> 78 us  [shards(): pl.pallas_call(kernel, out_shape=jax.ShapeDtypeStruct((1, BL, COLS), BF16...]
where the time goes in v3:
time: 80.1 us; the launch traced here: 79.5 us
  Pallas kernels  78 us (97%)
  local copies, waits for them, and re-layouts  1.47 us (2%)
    pallas_call x1, Pallas kernels, shards(): pl.pallas_call(kernel, out_shape=jax.ShapeDtypeStruct((1, BL, COLS), BF16...  78 us

profile of v3, /device:TPU:6, one launch (start us, length us, event | category | flops | bytes accessed | tf_op | source)
XLA Modules:
  0.0 79.5 jit_solution(12730556202391674154)
XLA Ops:
  0.0 78.0 %shard_map.82 = bf16[1,64,512]{2,1,0:T(8,128)(2,1)} custom-call(s32[2,1,32]{2,1,0:T(1,128)} %bitcast.3, s32[8]{0:T(128)} %plen_h.1, s32[2,32]{1,0:T(2,128)} %rlen_h.1, bf16[1,64,5120]{2,1,0:T(8,128)(2,1)} %hid_h.1, bf16[1,64,5120]{2,1,0:T(8,128)(2,1)} %car_h.1, bf16[1,160,512]{2,1,0:T(8,128)(2,1)} %w_h.1, bf16[1,64,256]{2,1,0:T(8,128)(2,1)} %rc_h.1, ...), custom_call_target="tpu_custom_call" | custom-call | tf_op jit(solution)/shard_map/pallas_call | solution.py:574
  78.0 1.5 %copy.11 = bf16[1,64,512]{2,1,0:T(8,128)(2,1)} copy(bf16[1,64,512]{2,1,0:T(8,128)(2,1)} %shard_map.82) | data formatting | bytes 131072

commit v4 on v3

--- a/solution.py
+++ b/solution.py
@@ -418,7 +418,7 @@
             from_x.at[n, ry % NY, :, lanes],
             ox_s.at[n, ry % NY, w],
             ox_r.at[n, ry % NY, w],
-            xm if n == 2 else x2 if n == 0 and abs(ry) > 2 else xp,
+            xm if n == 2 else x2 if n == 0 and abs(ry) > 1 else xp,
         )
 
     def y_hop(arm, k, w):
@@ -433,7 +433,7 @@
 
     def first(ry):
         for w, cols in enumerate(widths(ry)):
-            for rx, n in ((2, 0), (3, 2), (1, 1))[: 3 if abs(ry) > 2 else 2]:
+            for rx, n in ((2, 0), (3, 2), (1, 1))[: 3 if abs(ry) > 1 else 2]:
                 put(slot(rx, ry), cols, part_of(own.at[slot(rx, ry)], cols))
                 go(x_hop(n, ry, w))
 
@@ -445,7 +445,7 @@
             go(x_hop(1, ry, w))
 
     def joined(ry, w, cols):
-        hops = (2, 1, 0) if abs(ry) > 2 else (2, 1)
+        hops = (2, 1, 0) if abs(ry) > 1 else (2, 1)
         for n in hops:
             x_hop(n, ry, w).wait_recv()
         return merge(
@@ -496,10 +496,8 @@
     attend(-2)
     first(-2)
     on(3, 1, 3, 2)
-    second(2)
     attend(-3)
     first(-3)
-    second(-2)
     attend(3)
     first(3)
     on(4, 0)

time: 80.1 us -> 82.2 us (1.026)
  Pallas kernels: 78 us -> 80.6 us
    pallas_call x1, Pallas kernels: 78 us -> 80.6 us  [shards(): pl.pallas_call(kernel, out_shape=jax.ShapeDtypeStruct((1, BL, COLS), BF16...]
where the time goes in v4:
time: 82.2 us; the launch traced here: 82 us
  Pallas kernels  80.6 us (98%)
  local copies, waits for them, and re-layouts  1.47 us (2%)
    pallas_call x1, Pallas kernels, shards(): pl.pallas_call(kernel, out_shape=jax.ShapeDtypeStruct((1, BL, COLS), BF16...  80.6 us

profile of v4, /device:TPU:6, one launch (start us, length us, event | category | flops | bytes accessed | tf_op | source)
XLA Modules:
  0.0 82.0 jit_solution(9853474129941801422)
XLA Ops:
  0.0 80.6 %shard_map.82 = bf16[1,64,512]{2,1,0:T(8,128)(2,1)} custom-call(s32[2,1,32]{2,1,0:T(1,128)} %bitcast.3, s32[8]{0:T(128)} %plen_h.1, s32[2,32]{1,0:T(2,128)} %rlen_h.1, bf16[1,64,5120]{2,1,0:T(8,128)(2,1)} %hid_h.1, bf16[1,64,5120]{2,1,0:T(8,128)(2,1)} %car_h.1, bf16[1,160,512]{2,1,0:T(8,128)(2,1)} %w_h.1, bf16[1,64,256]{2,1,0:T(8,128)(2,1)} %rc_h.1, ...), custom_call_target="tpu_custom_call" | custom-call | tf_op jit(solution)/shard_map/pallas_call | solution.py:572
  80.6 1.5 %copy.11 = bf16[1,64,512]{2,1,0:T(8,128)(2,1)} copy(bf16[1,64,512]{2,1,0:T(8,128)(2,1)} %shard_map.82) | data formatting | bytes 131072
